TPU v7x, 32 devices: a whole 2x2x4 slice. The times are simulated.
32 devices in a mesh: grp: 2 (over y), feat: 4 (over z), tgt: 2 (over x), lay: 2 (over core).
Axes of the slice: x: 2, y: 2, z: 4, core: 2. Of those that a mesh axis runs over, the one named last changes fastest.
Arguments:
- decoder: bfloat16 [2, 32768, 4608], P('lay', 'feat', 'tgt'), may hold values from -6 to 6
- value_weight: bfloat16 [2, 1024, 4608], P('lay', 'feat', 'tgt'), may hold values from -0.09375 to 0.09375
- out_weight: bfloat16 [2, 2048, 4608], P('lay', 'feat', 'tgt'), may hold values from -0.09375 to 0.09375
- target_enc: bfloat16 [2, 512, 4608], P('lay', 'grp', 'tgt'), parts along dimension 1, may hold values from -6 to 6
- target_pos: int32 [2, 512], P('lay', 'grp'), parts along dimension 1, may hold values from 0 to 31
- attention: float32 [2, 32, 32, 32], P('lay', 'grp', 'feat'), parts along dimension 1, may hold values from 0.005 to 0.05
- norm_gain: float32 [2, 3, 4608], P('lay', None, 'tgt'), may hold values from 0.1 to 1.9
- norm_rstd: float32 [2, 6, 32], P('lay', 'grp'), parts along dimension 1, may hold values from 0.5 to 2
- source_owner: int32 [8192, 1], P(('grp', 'feat')), parts along dimension 0, may hold values from 0 to 3; in each aligned block of 1024 rows (0 to 1023, 1024 to 2047, ...) at most 512 rows name the same one
- source_row: int32 [8192], P(('grp', 'feat')), parts along dimension 0, may hold values from 0 to 8191
- source_act: float32 [8192], P(('grp', 'feat')), parts along dimension 0, may hold values from 0.25 to 2
- source_valid: int32 [8192], P(('grp', 'feat')), parts along dimension 0, may hold values 0 or 1
Outputs:
- edges: bfloat16 [2, 512, 4096], P('lay', ('grp', 'tgt'), 'feat'), parts along dimension 1
There are 2 independent parts, one for each index of `grp`. A program takes and returns all parts, laid end to end along the dimension named above; an argument that names none is the same for every part. Nothing has to cross between parts.
Inputs may be any that keep to these rules, and one draw needn't show every extreme that they name: `source_owner`: in each aligned block of 1024 slots (the source slots of one index of feat), no shard is named by more than 512 slots, a bound that some block reaches.
All inputs are finite; a program needn't handle non-finite values. No bound on the sum of `source_valid` on one device may be relied on, other than what follows from the above.
Results may differ from a plain program's by a relative error of at most 0.012.
Values may be sent and summed in bfloat16 or wider, within the bound.
A program may use at most 192 MiB of HBM per device.

v0:
```python
import jax
import jax.numpy as jnp
from jax import lax
from jax.sharding import PartitionSpec as P

HEADS = 16
KV = 8
HD = 128
K = 128


def on_device(
    decoder,
    value_weight,
    out_weight,
    target_enc,
    target_pos,
    attention,
    norm_gain,
    norm_rstd,
    source_owner,
    source_row,
    source_act,
    source_valid,
):
    n_feat = lax.axis_size("feat")
    shard = decoder[0]
    slot_count = source_row.shape[0]
    capacity = max(2, 2 * slot_count // n_feat)
    gains = norm_gain[0]
    positions = target_pos[0]
    targets = positions.shape[0]
    owners = source_owner[:, 0]
    member = (owners[:, None] == jnp.arange(n_feat, dtype=jnp.int32)[None, :]).astype(jnp.int32)
    ranks = jnp.sum((jnp.cumsum(member, axis=0) - 1) * member, axis=1)
    asked_rows = jnp.zeros((n_feat, capacity), jnp.int32).at[owners, ranks].set(source_row)
    flat_slot = owners * capacity + ranks
    gained_values = (value_weight[0].astype(jnp.float32) * gains[2]).astype(jnp.bfloat16)
    replies = lax.all_to_all(
        jnp.take(
            shard,
            lax.all_to_all(asked_rows, "feat", split_axis=0, concat_axis=0, tiled=True),
            axis=0,
        ),
        "feat",
        split_axis=0,
        concat_axis=0,
        tiled=True,
    )
    slot_rows = jnp.take(replies.reshape(n_feat * capacity, replies.shape[2]), flat_slot, axis=0)
    projected = jnp.dot(
        slot_rows,
        lax.all_gather(gained_values, "feat", axis=0, tiled=True).T,
        preferred_element_type=jnp.float32,
    ).astype(jnp.bfloat16)
    rstd_table = norm_rstd[0]
    tokens_all = rstd_table.shape[1]
    pos_table = (positions[:, None] == jnp.arange(tokens_all, dtype=jnp.int32)[None, :]).astype(
        jnp.float32
    )
    target_scale = jnp.dot(
        pos_table, rstd_table[0] * rstd_table[1], precision=lax.Precision.HIGHEST
    )
    enc_scaled = (target_enc[0].astype(jnp.float32) * gains[0] * gains[1]).astype(jnp.bfloat16)
    partial_heads = jnp.dot(enc_scaled, out_weight[0].T, preferred_element_type=jnp.float32)
    summed_heads = lax.psum(partial_heads, "tgt")
    heads_local = (summed_heads * target_scale[:, None]).astype(jnp.bfloat16)
    heads_back = lax.all_gather(heads_local, "feat", axis=1, tiled=True)
    attn_local = attention[0]
    tok_dev = attn_local.shape[1]
    group = HEADS // KV
    chosen = jnp.einsum("htq,fq->htf", attn_local, pos_table, precision=lax.Precision.HIGHEST)
    first_token = lax.axis_index("feat") * tok_dev
    key_tokens = first_token + jnp.arange(tok_dev, dtype=jnp.int32)
    causal = key_tokens[None, :, None] <= positions[None, None, :]
    chosen = jnp.where(causal, chosen, jnp.zeros_like(chosen))
    head_groups = heads_back.astype(jnp.float32).reshape(targets, KV, group, HD)
    weighted = jnp.einsum(
        "kgtf,fkgc->tfkc", chosen.reshape(KV, group, tok_dev, targets), head_groups
    )
    weighted = weighted.reshape(tok_dev, targets, KV * HD).astype(jnp.bfloat16)
    token_rows = projected.reshape(tok_dev, K, KV * HD)
    own_targets = targets // lax.axis_size("tgt")
    terms = jnp.einsum("tfc,tkc->ftk", weighted, token_rows, preferred_element_type=jnp.float32)
    scores = lax.psum_scatter(
        terms.reshape(lax.axis_size("tgt") * own_targets, tok_dev * K),
        "tgt",
        scatter_dimension=0,
        tiled=True,
    )
    local_rstd = lax.dynamic_slice_in_dim(rstd_table[2], first_token, tok_dev)
    source_scale = jnp.repeat(local_rstd, K) * source_act * source_valid.astype(jnp.float32)
    return (scores * source_scale[None, :]).astype(jnp.bfloat16)[None]


def solution(mesh):
    in_specs = (
        P("lay", "feat", "tgt"),
        P("lay", "feat", "tgt"),
        P("lay", "feat", "tgt"),
        P("lay", "grp", "tgt"),
        P("lay", "grp"),
        P("lay", "grp", "feat", None),
        P("lay", None, "tgt"),
        P("lay", "grp", None),
        P(("grp", "feat"), None),
        P(("grp", "feat")),
        P(("grp", "feat")),
        P(("grp", "feat")),
    )
    out_specs = P("lay", ("grp", "tgt"), "feat")
    return jax.shard_map(
        on_device, mesh=mesh, in_specs=in_specs, out_specs=out_specs, check_vma=False
    )
```

profile of v0, /device:TPU:0, one launch (start us, length us, event | category | flops | bytes accessed | tf_op | source)
XLA Modules:
  0.0 492.4 jit_solution(17582240208231121530)
XLA Ops:
  6.5 0.0 copy-start
  6.5 0.8 fusion.24
  7.4 1.1 reduce-window.6
  8.5 0.2 slice_reduce_fusion
  8.7 0.2 reduce-window.9
  8.9 0.1 add_bitcast_fusion
  9.0 0.7 fusion.21
  9.7 0.7 compare_select_fusion.1
  10.4 0.7 multiply_reduce_fusion
  11.1 0.8 and_reduce_fusion
  11.9 4.5 scatter_custom_fusion
  16.4 11.7 %all_to_all.20 = s32[4,1,512]{2,1,0:T(1,128)S(1)} all-to-all(s32[4,1,512]{2,1,0:T(1,128)S(1)} %bitcast.86), channel_id=1, replica_groups=mesh['grp'=2,'feat'=4,'tgt'=2,'lay'=2] {'feat'}, dimensions={0} | all-to-all | bytes 16384 | tf_op jit(solution)/shard_map/all_to_all | solution.py:42
  28.1 100.5 %gather_fusion = bf16[2048,2304]{1,0:T(8,128)(2,1)} fusion(bf16[8192,2304]{1,0:T(8,128)(2,1)} %bitcast.75, s32[2048]{0:T(1024)S(1)} %broadcast_clamp_fusion), kind=kCustom, calls=%fused_computation | custom fusion | bytes 18882560 | tf_op jit(solution)/shard_map/jit(_take)/gather | solution.py:40
  128.6 8.3 %broadcast_select_fusion = bf16[4,512,2304]{2,1,0:T(8,128)(2,1)} fusion(bf16[4,512,2304]{2,1,0:T(8,128)(2,1)} %bitcast.76, pred[4,512]{1,0:T(4,128)(4,1)S(1)} %compare_and_fusion), kind=kLoop, calls=%fused_computation.3 | loop fusion | flops 4718592 | bytes 18876416 | tf_op jit(solution)/shard_map/jit(_take)/select_n | solution.py:40
  136.9 5.8 %all-to-all-start.1 = ((bf16[4,512,2304]{2,1,0:T(8,128)(2,1)}), bf16[4,512,2304]{2,1,0:T(8,128)(2,1)}, u32[]{:S(2)}, u32[]{:S(2)}) async-start(bf16[4,512,2304]{2,1,0:T(8,128)(2,1)} %broadcast_select_fusion), calls=%async_computation.1 | async-start | bytes 18874368 | tf_op jit(solution)/shard_map/all_to_all | solution.py:39
  142.7 0.0 copy-start.3
  142.7 0.0 all-reduce.2.cloned.1.call-start
  142.7 0.9 slice_reduce_fusion.2
  143.6 0.0 copy-done
  143.7 2.9 fusion.4
  146.5 0.0 copy-start.6
  146.6 0.0 copy-start.4
  146.6 0.0 copy-start.5
  146.6 0.0 all-reduce.2.cloned.1.call-update
  146.6 0.0 all-gather.5.cloned.1.call-start
  146.6 0.8 fusion.18
  147.5 28.3 %all-reduce.2.cloned.1.call-done = f32[256,512]{1,0:T(8,128)} async-done(((f32[256,512]{1,0:T(8,128)}), f32[256,512]{1,0:T(8,128)}) %all-reduce.2.cloned.1.call-update) | async-done | bytes 524304 | tf_op jit(solution)/shard_map/psum | solution.py:66
  175.8 1.8 multiply_convert_fusion.2
  177.6 0.0 all-gather.5.cloned.1.call-update
  177.6 0.0 all-gather.3.cloned.1.call-start
  177.7 0.0 copy-done.3
  177.7 1.2 fusion.3
  178.9 0.0 all-gather.3.cloned.1.call-update
  178.9 0.2 reduce-scatter.2.cloned.1.call-start
  179.2 0.0 copy-done.6
  179.2 0.1 broadcast_compare_fusion
  179.3 0.0 copy-done.4
  179.3 0.2 fusion.14
  179.5 1.0 copy.27
  180.5 0.0 copy-done.5
  180.5 41.6 %all-gather.5.cloned.1.call-done = bf16[256,2048]{1,0:T(8,128)(2,1)} async-done(((bf16[256,512]{1,0:T(8,128)(2,1)}), bf16[256,2048]{1,0:T(8,128)(2,1)}) %all-gather.5.cloned.1.call-update) | async-done | bytes 1048592 | tf_op jit(solution)/shard_map/all_gather | solution.py:68
  222.1 1.8 reshape.167
  223.9 4.2 convert_bitcast_fusion
  228.1 6.9 %copy.23 = bf16[8,256,8,128]{1,3,2,0:T(8,128)(2,1)} copy(bf16[8,256,8,128]{3,0,2,1:T(8,128)(2,1)} %convert_bitcast_fusion) | data formatting | bytes 8388608 | tf_op jit(solution)/shard_map/convert_element_type | solution.py:81
  235.0 202.8 %all-to-all-done.1 = bf16[4,512,2304]{2,1,0:T(8,128)(2,1)} async-done(((bf16[4,512,2304]{2,1,0:T(8,128)(2,1)}), bf16[4,512,2304]{2,1,0:T(8,128)(2,1)}, u32[]{:S(2)}, u32[]{:S(2)}) %all-to-all-start.1) | async-done | bytes 9437216 | tf_op jit(solution)/shard_map/all_to_all | solution.py:39
  437.8 14.7 %gather_fusion.1 = bf16[1024,2304]{1,0:T(8,128)(2,1)} fusion(bf16[2048,2304]{1,0:T(8,128)(2,1)} %bitcast.9, s32[1024]{0:T(1024)S(1)} %broadcast_clamp_fusion.1), kind=kCustom, calls=%fused_computation.1 | custom fusion | bytes 9441280 | tf_op jit(solution)/shard_map/jit(_take)/gather | solution.py:50
  452.4 0.0 all-gather.3.cloned.1.call-done
  452.4 8.7 %fusion.7 = bf16[1024,1024]{1,0:T(8,128)(2,1)S(1)} fusion(bf16[1024,2304]{1,0:T(8,128)(2,1)} %all-gather.3.cloned.1.call-done, bf16[1024,2304]{1,0:T(8,128)(2,1)} %gather_fusion.1, pred[1024]{0:T(1024)(128)(4,1)S(1)} %get-tuple-element.8), kind=kOutput, calls=%fused_computation.14 | convolution fusion | flops 4835246080 | bytes 11535360 | tf_op jit(solution)/shard_map/dot_general | solution.py:51
  461.2 0.0 copy-done.2
  461.2 0.0 slice-start
  461.2 0.0 copy-start.7
  461.2 0.0 copy-start.8
  461.2 0.0 copy-start.1
  461.2 0.7 fusion.31
  462.0 1.3 copy.25
  463.3 0.0 reduce-scatter.2.cloned.1.call-update
  463.3 0.0 slice-done
  463.3 0.1 dynamic-slice_bitcast_fusion
  463.4 0.0 copy-done.7
  463.4 0.0 copy-done.8
  463.4 0.1 fusion.25
  463.5 20.6 %reduce-scatter.2.cloned.1.call-done = f32[128,1024]{1,0:T(8,128)} async-done(((f32[256,1024]{1,0:T(8,128)}), f32[128,1024]{1,0:T(8,128)}) %reduce-scatter.2.cloned.1.call-update) | async-done | bytes 524304 | tf_op jit(solution)/shard_map/reduce_scatter | solution.py:85
  484.1 1.8 fusion.15
  485.9 0.0 copy-done.1
  (8 shorter events, 0.1 us)
Async XLA Ops:
  6.5 137.1 %copy-start = (bf16[1,512,2304]{2,1,0:T(8,128)(2,1)S(1)}, bf16[1,512,2304]{2,1,0:T(8,128)(2,1)}, u32[]{:S(2)}) copy-start(bf16[1,512,2304]{2,1,0:T(8,128)(2,1)} %param.14) | copy-start | bytes 7077892
  136.9 300.9 %all-to-all-start.1 = ((bf16[4,512,2304]{2,1,0:T(8,128)(2,1)}), bf16[4,512,2304]{2,1,0:T(8,128)(2,1)}, u32[]{:S(2)}, u32[]{:S(2)}) async-start(bf16[4,512,2304]{2,1,0:T(8,128)(2,1)} %broadcast_select_fusion), calls=%async_computation.1 | async-start | bytes 18874368 | tf_op jit(solution)/shard_map/all_to_all | solution.py:39
  142.7 35.0 %copy-start.3 = (bf16[1,256,2304]{2,1,0:T(8,128)(2,1)S(1)}, bf16[1,256,2304]{2,1,0:T(8,128)(2,1)}, u32[]{:S(2)}) copy-start(bf16[1,256,2304]{2,1,0:T(8,128)(2,1)} %param.13) | copy-start | bytes 3538948
  142.7 33.1 %all-reduce.2.cloned.1.call-start = ((), (), s32[]{:S(2)}) async-start(), calls=%async_computation.4 | async-start | bytes 1048576 | tf_op jit(solution)/shard_map/psum | solution.py:66
  146.5 32.6 %copy-start.6 = (s32[1,256]{1,0:T(1,128)S(1)}, s32[1,256]{1,0:T(1,128)}, u32[]{:S(2)}) copy-start(s32[1,256]{1,0:T(1,128)} %param.16) | copy-start | bytes 3076
  146.6 32.7 %copy-start.4 = (f32[1,16,8,32]{3,2,1,0:T(8,128)S(1)}, f32[1,16,8,32]{3,2,1,0:T(8,128)}, u32[]{:S(2)}) copy-start(f32[1,16,8,32]{3,2,1,0:T(8,128)} %param.17) | copy-start | bytes 49156
  146.6 33.9 %copy-start.5 = (s32[1024,1]{0,1:T(1,128)S(1)}, s32[1024,1]{0,1:T(1,128)}, u32[]{:S(2)}) copy-start(s32[1024,1]{0,1:T(1,128)} %param.20) | copy-start | bytes 12292
  146.6 75.5 %all-gather.5.cloned.1.call-start = ((), (), s32[]{:S(2)}) async-start(), calls=%async_computation.5 | async-start | bytes 1310720 | tf_op jit(solution)/shard_map/all_gather | solution.py:68
  177.6 274.8 %all-gather.3.cloned.1.call-start = ((), (), s32[]{:S(2)}) async-start(), calls=%async_computation.3 | async-start | bytes 5898240 | tf_op jit(solution)/shard_map/all_gather | solution.py:53
  178.9 305.2 %reduce-scatter.2.cloned.1.call-start = ((), (), s32[]{:S(2)}) async-start(), calls=%async_computation.6 | async-start | bytes 1572864 | tf_op jit(solution)/shard_map/reduce_scatter | solution.py:85
  452.4 8.8 %copy-start.2 = (bf16[8,256,8,128]{1,3,2,0:T(8,128)(2,1)S(1)}, bf16[8,256,8,128]{1,3,2,0:T(8,128)(2,1)}, u32[]{:S(2)}) copy-start(bf16[8,256,8,128]{1,3,2,0:T(8,128)(2,1)} %copy.23) | copy-start | bytes 12582916
  461.2 2.1 slice-start
  461.2 2.2 copy-start.7
  461.2 2.2 copy-start.8
  461.2 24.7 %copy-start.1 = (bf16[1,512,2304]{2,1,0:T(8,128)(2,1)S(1)}, bf16[1,512,2304]{2,1,0:T(8,128)(2,1)}, u32[]{:S(2)}) copy-start(bf16[1,512,2304]{2,1,0:T(8,128)(2,1)} %param.14) | copy-start | bytes 7077892
Sparse Core Ops, SparseCore 0:
  146.7 29.0 all-reduce.1
  177.7 44.3 all-gather.4
  223.7 216.7 all-gather.2
  463.4 20.6 reduce-scatter.1
where the time goes:
time: 492 us
  waiting for transfers between devices  293 us (60%)
  local copies, waits for them, and re-layouts  132 us (27%)
  other arithmetic  18.5 us (4%)
  matrix products  17.5 us (4%)
  between operations  13.3 us (3%)
  blocking collectives  11.7 us (2%)
  starting transfers between devices  6.15 us (1%)
    all_to_all x1, waiting for transfers between devices, on_device(): lax.all_to_all(jnp.take(shard, lax.all_to_all(asked_rows, 'feat', split_a...  203 us
    gather x1, local copies, waits for them, and re-layouts, on_device(): jnp.take(shard, lax.all_to_all(asked_rows, 'feat', split_axis=0, concat_a...  100 us
    all_gather x1, waiting for transfers between devices, on_device(): heads_back = lax.all_gather(heads_local, 'feat', axis=1, tiled=True)  41.6 us
    psum x1, waiting for transfers between devices, on_device(): summed_heads = lax.psum(partial_heads, 'tgt')  28.3 us
    reduce_scatter x1, waiting for transfers between devices, on_device(): lax.psum_scatter(terms.reshape(lax.axis_size('tgt') * own_targets, tok_de...  20.6 us
    gather x1, local copies, waits for them, and re-layouts, on_device(): jnp.take(replies.reshape(n_feat * capacity, replies.shape[2]), flat_slot,...  14.7 us
    all_to_all x1, blocking collectives, on_device(): lax.all_to_all(asked_rows, 'feat', split_axis=0, concat_axis=0, tiled=True)  11.7 us
  transfers between devices with their start and end apart: 5, of which 4 were waited for; matrix products, arithmetic and copies ran while one was open for 7% of the time, Pallas kernels for 0%

commit v1 on v0

v1 whole, which is shorter than its diff:
```python
import functools
import jax
import jax.numpy as jnp
from jax import lax
from jax.experimental import pallas as pl
from jax.experimental.pallas import tpu as pltpu
from jax.sharding import PartitionSpec as P

HEADS = 16
KV = 8
HD = 128
K = 128


def score_kernel(rows_ref, values_ref, heads_ref, picked_ref, token_ref, out_ref):
    group = HEADS // KV
    projected = lax.dot_general(
        values_ref[...],
        rows_ref[...],
        (((1,), (1,)), ((), ())),
        preferred_element_type=jnp.float32,
    ).astype(jnp.bfloat16)
    tokens = picked_ref.shape[2]
    slots = token_ref.shape[1]
    which = lax.broadcasted_iota(jnp.int32, (tokens, slots), 0) == token_ref[...]
    which = jnp.where(which, 1.0, 0.0).astype(jnp.bfloat16)
    total = jnp.zeros(out_ref.shape, jnp.float32)
    for head in range(HEADS):
        kv = head // group
        match = jnp.dot(
            heads_ref[:, head * HD : (head + 1) * HD],
            projected[kv * HD : (kv + 1) * HD],
            preferred_element_type=jnp.float32,
        )
        weight = jnp.dot(picked_ref[head], which, preferred_element_type=jnp.float32)
        total = total + match * weight
    out_ref[...] = total.astype(jnp.bfloat16)


def owner_scores(rows, values, heads, picked, tokens_of_slot):
    slots, width = rows.shape
    targets = heads.shape[0]
    block = 256
    return pl.pallas_call(
        score_kernel,
        grid=(slots // block,),
        in_specs=[
            pl.BlockSpec((block, width), lambda i: (i, 0)),
            pl.BlockSpec(values.shape, lambda i: (0, 0)),
            pl.BlockSpec(heads.shape, lambda i: (0, 0)),
            pl.BlockSpec(picked.shape, lambda i: (0, 0, 0)),
            pl.BlockSpec((1, block), lambda i: (0, i)),
        ],
        out_specs=pl.BlockSpec((targets, block), lambda i: (0, i)),
        out_shape=jax.ShapeDtypeStruct((targets, slots), jnp.bfloat16),
        compiler_params=pltpu.CompilerParams(vmem_limit_bytes=48 * 1024 * 1024),
    )(rows, values, heads, picked, tokens_of_slot)


def place_kernel(replies_ref, place_ref, scale_ref, out_ref):
    capacity = replies_ref.shape[2]
    slots = place_ref.shape[1]
    total = jnp.zeros(out_ref.shape, jnp.float32)
    spots = lax.broadcasted_iota(jnp.int32, (capacity, slots), 0)
    for owner in range(replies_ref.shape[0]):
        which = jnp.where(spots + owner * capacity == place_ref[...], 1.0, 0.0)
        total = total + jnp.dot(
            replies_ref[owner], which.astype(jnp.bfloat16), preferred_element_type=jnp.float32
        )
    out_ref[...] = (total * scale_ref[...]).astype(jnp.bfloat16)


def on_device(
    decoder,
    value_weight,
    out_weight,
    target_enc,
    target_pos,
    attention,
    norm_gain,
    norm_rstd,
    source_owner,
    source_row,
    source_act,
    source_valid,
):
    n_feat = lax.axis_size("feat")
    n_tgt = lax.axis_size("tgt")
    me_tgt = lax.axis_index("tgt")
    shard = decoder[0]
    shard_rows = shard.shape[0]
    slot_count = source_row.shape[0]
    capacity = max(2, 2 * slot_count // n_feat)
    gains = norm_gain[0]
    positions = target_pos[0]
    targets = positions.shape[0]
    owners = source_owner[:, 0]

    def shifted(x, step):
        return lax.ppermute(x, "tgt", [(i, (i + step) % n_tgt) for i in range(n_tgt)])

    gained_values = (value_weight[0].astype(jnp.float32) * gains[2]).astype(jnp.bfloat16)
    values = lax.all_gather(gained_values, "feat", axis=0, tiled=True)

    member = (owners[:, None] == jnp.arange(n_feat, dtype=jnp.int32)[None, :]).astype(jnp.int32)
    ranks = jnp.sum((jnp.cumsum(member, axis=0) - 1) * member, axis=1)
    flat_slot = owners * capacity + ranks
    token_here = jnp.arange(slot_count, dtype=jnp.int32) // K
    asked = jnp.sum(
        jnp.where(
            flat_slot[None, :] == jnp.arange(n_feat * capacity, dtype=jnp.int32)[:, None],
            (token_here * shard_rows + source_row)[None, :],
            0,
        ),
        axis=1,
    )
    asked = lax.all_to_all(
        asked.reshape(n_feat, capacity), "feat", split_axis=0, concat_axis=0, tiled=True
    )
    rows = shard.at[(asked % shard_rows).reshape(-1)].get(mode="promise_in_bounds")
    tok_dev = attention.shape[2]
    tokens_of_slot = asked // shard_rows + (
        jnp.arange(n_feat, dtype=jnp.int32) * tok_dev
    )[:, None]

    rstd_table = norm_rstd[0]
    tokens_all = rstd_table.shape[1]
    pos_table = (positions[:, None] == jnp.arange(tokens_all, dtype=jnp.int32)[None, :]).astype(
        jnp.float32
    )
    target_scale = jnp.dot(
        pos_table, rstd_table[0] * rstd_table[1], precision=lax.Precision.HIGHEST
    )
    enc_scaled = (target_enc[0].astype(jnp.float32) * gains[0] * gains[1]).astype(jnp.bfloat16)
    partial_heads = jnp.dot(enc_scaled, out_weight[0].T, preferred_element_type=jnp.float32)
    summed_heads = partial_heads
    for step in range(1, n_tgt):
        summed_heads = summed_heads + shifted(partial_heads, step)
    heads_local = (summed_heads * target_scale[:, None]).astype(jnp.bfloat16)
    heads_back = lax.all_gather(heads_local, "feat", axis=1, tiled=True)

    attn_all = lax.all_gather(attention[0].astype(jnp.bfloat16), "feat", axis=1, tiled=True)
    chosen = jnp.einsum(
        "fq,htq->hft",
        pos_table.astype(jnp.bfloat16),
        attn_all,
        preferred_element_type=jnp.float32,
    )
    causal = jnp.arange(tokens_all, dtype=jnp.int32)[None, :] <= positions[:, None]
    picked = jnp.where(causal[None], chosen, 0.0).astype(jnp.bfloat16)

    raw = owner_scores(rows, values, heads_back, picked, tokens_of_slot.reshape(1, -1))
    own_targets = targets // n_tgt

    def part(of):
        return lax.dynamic_slice_in_dim(raw, of * own_targets, own_targets)

    scores = part(me_tgt).astype(jnp.float32)
    for step in range(1, n_tgt):
        scores = scores + shifted(part((me_tgt + step) % n_tgt), step).astype(jnp.float32)
    replies = lax.all_to_all(
        scores.astype(jnp.bfloat16).reshape(own_targets, n_feat, capacity).transpose(1, 0, 2),
        "feat",
        split_axis=0,
        concat_axis=0,
        tiled=True,
    )
    local_rstd = lax.dynamic_slice_in_dim(
        rstd_table[2], lax.axis_index("feat") * tok_dev, tok_dev
    )
    source_scale = jnp.repeat(local_rstd, K) * source_act * source_valid.astype(jnp.float32)
    return pl.pallas_call(
        place_kernel,
        out_shape=jax.ShapeDtypeStruct((own_targets, slot_count), jnp.bfloat16),
        compiler_params=pltpu.CompilerParams(vmem_limit_bytes=32 * 1024 * 1024),
    )(replies, flat_slot[None, :], source_scale[None, :])[None]


def solution(mesh):
    in_specs = (
        P("lay", "feat", "tgt"),
        P("lay", "feat", "tgt"),
        P("lay", "feat", "tgt"),
        P("lay", "grp", "tgt"),
        P("lay", "grp"),
        P("lay", "grp", "feat", None),
        P("lay", None, "tgt"),
        P("lay", "grp", None),
        P(("grp", "feat"), None),
        P(("grp", "feat")),
        P(("grp", "feat")),
        P(("grp", "feat")),
    )
    out_specs = P("lay", ("grp", "tgt"), "feat")
    return jax.shard_map(
        on_device, mesh=mesh, in_specs=in_specs, out_specs=out_specs, check_vma=False
    )
```

time: 492 us -> 236 us (0.48)
  waiting for transfers between devices: 293 us -> 37.7 us
  Pallas kernels: 0 us -> 40.7 us
  local copies, waits for them, and re-layouts: 132 us -> 101 us
  matrix products: 17.5 us -> 4.42 us
  other arithmetic: 18.5 us -> 9.42 us
  starting transfers between devices: 6.15 us -> 12.8 us
    all_to_all x1 -> x2, waiting for transfers between devices: 203 us -> 13.3 us  [the longest x1 13.3 us: on_device(): lax.all_to_all(scores.astype(jnp.bfloat16).reshape(own_targets, n_feat, c...]
    all_gather x1, waiting for transfers between devices: 41.6 us -> 0.02 us  [on_device(): heads_back = lax.all_gather(heads_local, 'feat', axis=1, tiled=True)]
    pallas_call x0 -> x2, Pallas kernels: none -> 40.7 us  [the longest x1 39.3 us: owner_scores(): pl.pallas_call(score_kernel, grid=(slots // block,), in_specs=[pl.BlockSp...]
    psum x1 -> x0, waiting for transfers between devices: 28.3 us -> none  [on_device(): summed_heads = lax.psum(partial_heads, 'tgt')]
    ppermute x0 -> x2, waiting for transfers between devices: none -> 24.3 us  [shifted(): lax.ppermute(x, 'tgt', [(i, (i + step) % n_tgt) for i in range(n_tgt)])]
    gather x2 -> x1, local copies, waits for them, and re-layouts: 115 us -> 93.3 us  [on_device(): shard.at[(asked % shard_rows).reshape(-1)].get(mode='promise_in_bounds')]
    reduce_scatter x1 -> x0, waiting for transfers between devices: 20.6 us -> none  [on_device(): lax.psum_scatter(terms.reshape(lax.axis_size('tgt') * own_targets, tok_de...]
    all_gather x0 -> x1, blocking collectives: none -> 15 us  [on_device(): lax.all_gather(attention[0].astype(jnp.bfloat16), 'feat', axis=1, tiled=T...]
  transfers between devices with their start and end apart: 5 -> 6, of which waited for: 4 -> 3; matrix products, arithmetic and copies ran while one was open for 7% -> 44% of each run, Pallas kernels for 0% -> 0%
where the time goes in v1:
time: 236 us; the launch traced here: 235 us
  local copies, waits for them, and re-layouts  101 us (43%)
  Pallas kernels  40.7 us (17%)
  waiting for transfers between devices  37.7 us (16%)
  blocking collectives  15 us (6%)
  between operations  13.6 us (6%)
  starting transfers between devices  12.8 us (5%)
  other arithmetic  9.42 us (4%)
  matrix products  4.42 us (2%)
    gather x1, local copies, waits for them, and re-layouts, on_device(): shard.at[(asked % shard_rows).reshape(-1)].get(mode='promise_in_bounds')  93.3 us
    pallas_call x1, Pallas kernels, owner_scores(): pl.pallas_call(score_kernel, grid=(slots // block,), in_specs=[pl.BlockSp...  39.3 us
    ppermute x2, waiting for transfers between devices, shifted(): lax.ppermute(x, 'tgt', [(i, (i + step) % n_tgt) for i in range(n_tgt)])  24.3 us
    all_gather x1, blocking collectives, on_device(): lax.all_gather(attention[0].astype(jnp.bfloat16), 'feat', axis=1, tiled=T...  15 us
    all_to_all x1, waiting for transfers between devices, on_device(): lax.all_to_all(scores.astype(jnp.bfloat16).reshape(own_targets, n_feat, c...  13.3 us
    all_to_all x1, starting transfers between devices, on_device(): lax.all_to_all(asked.reshape(n_feat, capacity), 'feat', split_axis=0, con...  5.12 us
  transfers between devices with their start and end apart: 6, of which 3 were waited for; matrix products, arithmetic and copies ran while one was open for 44% of the time, Pallas kernels for 0%

profile of v1, /device:TPU:0, one launch (start us, length us, event | category | flops | bytes accessed | tf_op | source)
XLA Modules:
  0.0 234.7 jit_solution(7204716214922836366)
XLA Ops:
  6.5 0.0 copy-start
  6.5 0.0 all-gather.6.cloned.1.call-start
  6.5 1.0 slice_reduce_fusion.2
  7.5 0.8 copy-done
  8.2 0.0 copy-start.7
  8.3 0.0 copy-start.8
  8.3 0.0 copy-start.3
  8.3 2.2 fusion.1
  10.4 3.0 %collective-permute-start = (f32[256,512]{1,0:T(8,128)S(1)}, f32[256,512]{1,0:T(8,128)S(1)}, u32[]{:S(2)}, u32[]{:S(2)}) collective-permute-start(f32[256,512]{1,0:T(8,128)S(1)} %fusion.1), channel_id=1, source_target_pairs={{0,2},{2,0},{1,3},{3,1},{4,6},{6,4},{5,7},{7,5},{8,10},{10,8},{9,1... | collective-permute-start | bytes 1572872 | tf_op jit(solution)/shard_map/ppermute | solution.py:100
  13.4 0.0 copy-done.7
  13.4 0.0 copy-done.8
  13.4 0.1 fusion.9
  13.6 11.8 %collective-permute-done = f32[256,512]{1,0:T(8,128)S(1)} collective-permute-done((f32[256,512]{1,0:T(8,128)S(1)}, f32[256,512]{1,0:T(8,128)S(1)}, u32[]{:S(2)}, u32[]{:S(2)}) %collective-permute-start) | collective-permute-done | bytes 524320 | tf_op jit(solution)/shard_map/ppermute | solution.py:100
  25.4 0.0 copy-start.4
  25.4 0.8 multiply_convert_fusion.1
  26.2 0.0 all-gather.6.cloned.1.call-update
  26.2 0.0 all-gather.4.cloned.1.call-start
  26.3 0.0 copy-done.3
  26.3 1.2 fusion
  27.5 0.0 all-gather.4.cloned.1.call-update
  27.5 0.0 copy-done.4
  27.6 1.1 reduce-window.6
  28.7 0.2 slice_reduce_fusion
  28.9 0.2 reduce-window.9
  29.1 0.1 add_bitcast_fusion
  29.2 0.7 fusion.20
  29.9 1.5 select_reduce_fusion
  31.4 5.1 %all-to-all-start = ((s32[4,1,512]{2,1,0:T(1,128)}), s32[4,1,512]{2,1,0:T(1,128)S(1)}, u32[]{:S(2)}, u32[]{:S(2)}) async-start(s32[4,1,512]{2,1,0:T(1,128)} %bitcast.4), calls=%async_computation | async-start | bytes 16384 | tf_op jit(solution)/shard_map/all_to_all | solution.py:117
  36.5 0.7 iota_compare_fusion.1
  37.2 0.1 copy.23
  37.4 0.8 convert_element_type.66
  38.2 15.0 %all-gather = bf16[1,16,32,32]{3,2,1,0:T(8,128)(2,1)S(1)} all-gather(bf16[1,16,8,32]{3,2,1,0:T(8,128)(2,1)S(1)} %convert_element_type.66), channel_id=2, replica_groups=mesh['grp'=2,'feat'=4,'tgt'=2,'lay'=2] {'feat'}, dimensions={2}, use_global_device_ids=true | all-gather | bytes 40960 | tf_op jit(solution)/shard_map/all_gather | solution.py:142
  53.3 2.1 fusion.3.picked_ref
  55.4 0.1 broadcast_bitcast_fusion
  55.5 0.0 all-to-all-done
  55.5 93.3 %gather_fusion = bf16[2048,2304]{1,0:T(8,128)(2,1)} fusion(bf16[8192,2304]{1,0:T(8,128)(2,1)} %bitcast.64, s32[2048]{0:T(1024)S(1)} %broadcast_clamp_fusion), kind=kCustom, calls=%fused_computation | custom fusion | bytes 18882560 | tf_op jit(solution)/shard_map/gather | solution.py:120
  148.9 0.0 all-gather.6.cloned.1.call-done.heads_ref
  148.9 0.0 all-gather.4.cloned.1.call-done.values_ref
  148.9 0.0 copy-start.1
  148.9 1.2 copy-done.1
  150.2 0.0 copy-start.2
  150.2 1.2 copy-done.2
  151.4 39.3 %shard_map.118 = bf16[256,2048]{1,0:T(8,128)(2,1)S(1)} custom-call(bf16[2048,2304]{1,0:T(8,128)(2,1)} %gather_fusion, bf16[1024,2304]{1,0:T(8,128)(2,1)} %all-gather.4.cloned.1.call-done.values_ref, bf16[256,2048]{1,0:T(8,128)(2,1)S(1)} %copy-done.1, bf16[16,256,32]{2,1,0:T(8,128)(2,1)S(1)} %copy-done.2, s32[1,2048]{1,0:T(1,128)S(1)} %fusion.18.token_ref), custom_call_target="tpu_custom_call" | custom-call | tf_op jit(solution)/shard_map/pallas_call | solution.py:44
  190.7 0.8 constant_dynamic-slice_fusion
  191.5 1.1 collective-permute-start.1
  192.7 0.0 slice-start
  192.7 0.0 copy-start.5
  192.7 0.0 copy-start.6
  192.7 12.5 %collective-permute-done.1 = bf16[128,2048]{1,0:T(8,128)(2,1)} collective-permute-done((bf16[128,2048]{1,0:T(8,128)(2,1)}, bf16[128,2048]{1,0:T(8,128)(2,1)}, u32[]{:S(2)}, u32[]{:S(2)}) %collective-permute-start.1) | collective-permute-done | bytes 524320 | tf_op jit(solution)/shard_map/ppermute | solution.py:100
  205.2 2.0 add_convert_fusion
  207.2 1.3 copy.25
  208.5 1.0 copy.26
  209.5 3.5 %all-to-all-start.1 = ((bf16[4,128,512]{2,1,0:T(8,128)(2,1)}), bf16[4,128,512]{2,1,0:T(8,128)(2,1)S(1)}, u32[]{:S(2)}, u32[]{:S(2)}) async-start(bf16[4,128,512]{2,1,0:T(8,128)(2,1)} %bitcast.19), calls=%async_computation.1 | async-start | bytes 1048576 | tf_op jit(solution)/shard_map/all_to_all | solution.py:161
  213.0 0.0 slice-done
  213.0 0.1 fusion.25
  213.1 0.0 copy-done.5
  213.1 0.0 copy-done.6
  213.1 0.1 fusion.23
  213.2 13.3 %all-to-all-done.1.replies_ref = bf16[4,128,512]{2,1,0:T(8,128)(2,1)S(1)} async-done(((bf16[4,128,512]{2,1,0:T(8,128)(2,1)}), bf16[4,128,512]{2,1,0:T(8,128)(2,1)S(1)}, u32[]{:S(2)}, u32[]{:S(2)}) %all-to-all-start.1) | async-done | bytes 524320 | tf_op jit(solution)/shard_map/all_to_all | solution.py:161
  226.5 1.4 shard_map.119
  (8 shorter events, 0.1 us)
Async XLA Ops:
  6.5 1.7 copy-start
  6.5 142.4 %all-gather.6.cloned.1.call-start = ((), (), s32[]{:S(2)}) async-start(), calls=%async_computation.3 | async-start | bytes 1310720 | tf_op jit(solution)/shard_map/all_gather | solution.py:140
  8.2 5.2 %copy-start.7 = (s32[1,256]{1,0:T(1,128)S(1)}, s32[1,256]{1,0:T(1,128)}, u32[]{:S(2)}) copy-start(s32[1,256]{1,0:T(1,128)} %param.16) | copy-start | bytes 3076
  8.3 5.2 %copy-start.8 = (f32[1,3,32]{2,0,1:T(1,128)S(1)}, f32[1,3,32]{2,0,1:T(1,128)}, u32[]{:S(2)}) copy-start(f32[1,3,32]{2,0,1:T(1,128)} %param.19) | copy-start | bytes 1156
  8.3 18.0 %copy-start.3 = (bf16[1,256,2304]{2,1,0:T(8,128)(2,1)S(1)}, bf16[1,256,2304]{2,1,0:T(8,128)(2,1)}, u32[]{:S(2)}) copy-start(bf16[1,256,2304]{2,1,0:T(8,128)(2,1)} %param.13) | copy-start | bytes 3538948
  10.4 14.9 %collective-permute-start = (f32[256,512]{1,0:T(8,128)S(1)}, f32[256,512]{1,0:T(8,128)S(1)}, u32[]{:S(2)}, u32[]{:S(2)}) collective-permute-start(f32[256,512]{1,0:T(8,128)S(1)} %fusion.1), channel_id=1, source_target_pairs={{0,2},{2,0},{1,3},{3,1},{4,6},{6,4},{5,7},{7,5},{8,10},{10,8},{9,1... | collective-permute-start | bytes 1572872 | tf_op jit(solution)/shard_map/ppermute | solution.py:100
  25.4 2.2 copy-start.4
  26.2 122.7 %all-gather.4.cloned.1.call-start = ((), (), s32[]{:S(2)}) async-start(), calls=%async_computation.2 | async-start | bytes 5898240 | tf_op jit(solution)/shard_map/all_gather | solution.py:103
  31.4 24.1 %all-to-all-start = ((s32[4,1,512]{2,1,0:T(1,128)}), s32[4,1,512]{2,1,0:T(1,128)S(1)}, u32[]{:S(2)}, u32[]{:S(2)}) async-start(s32[4,1,512]{2,1,0:T(1,128)} %bitcast.4), calls=%async_computation | async-start | bytes 16384 | tf_op jit(solution)/shard_map/all_to_all | solution.py:117
  148.9 1.2 copy-start.1
  150.2 1.2 copy-start.2
  191.5 13.6 %collective-permute-start.1 = (bf16[128,2048]{1,0:T(8,128)(2,1)}, bf16[128,2048]{1,0:T(8,128)(2,1)}, u32[]{:S(2)}, u32[]{:S(2)}) collective-permute-start(bf16[128,2048]{1,0:T(8,128)(2,1)} %constant_dynamic-slice_fusion), channel_id=1, source_target_pairs={{0,2},{2,0},{1,3},{3,1},{4,6},{6,4},{5,7},{7,5},{8,10},{10,8},{9,1... | collective-permute-start | bytes 1572872 | tf_op jit(solution)/shard_map/ppermute | solution.py:100
  192.7 20.3 %slice-start = ((f32[1,3,32]{2,0,1:T(1,128)}), f32[1,1,32]{2,0,1:T(1,128)S(1)}, s32[]{:S(2)}) async-start(f32[1,3,32]{2,0,1:T(1,128)} %param.19), calls=%async_computation.4 | async-start | bytes 1024 | tf_op jit(solution)/shard_map/slice | solution.py:169
  192.7 20.4 %copy-start.5 = (f32[1024]{0:T(1024)S(1)}, f32[1024]{0:T(1024)}, u32[]{:S(2)}) copy-start(f32[1024]{0:T(1024)} %param.22) | copy-start | bytes 12292
  192.7 20.4 %copy-start.6 = (s32[1024]{0:T(1024)S(1)}, s32[1024]{0:T(1024)}, u32[]{:S(2)}) copy-start(s32[1024]{0:T(1024)} %param.23) | copy-start | bytes 12292
  209.5 16.9 %all-to-all-start.1 = ((bf16[4,128,512]{2,1,0:T(8,128)(2,1)}), bf16[4,128,512]{2,1,0:T(8,128)(2,1)S(1)}, u32[]{:S(2)}, u32[]{:S(2)}) async-start(bf16[4,128,512]{2,1,0:T(8,128)(2,1)} %bitcast.19), calls=%async_computation.1 | async-start | bytes 1048576 | tf_op jit(solution)/shard_map/all_to_all | solution.py:161
Sparse Core Ops, SparseCore 0:
  26.3 31.7 all-gather.5
  59.7 88.7 all-gather.3
